TPU v7x, 128 devices: a whole 4x4x4 slice. The times are simulated.
128 devices in a mesh: rows: 32 (over z, x, core), half: 4 (over y).
Axes of the slice: x: 4, y: 4, z: 4, core: 2. Of those that a mesh axis runs over, the one named last changes fastest.
Arguments:
- pair: bfloat16 [1024, 1024, 128], P('rows', 'half'), may hold values from -6 to 6
- pair_mask: int32 [1024, 1024], P('rows', 'half'), may hold values from 0 to 1, as said below
- gains: float32 [3, 128], replicated, may hold values from 0.1 to 1.9
- w_tri: bfloat16 [128, 640], replicated, may hold values from -0.5 to 0.5
- w_tri_out: bfloat16 [128, 128], replicated, may hold values from -0.5 to 0.5
- w_att: bfloat16 [128, 512], replicated, may hold values from -0.5 to 0.5
- w_bias: bfloat16 [128, 4], replicated, may hold values from -0.5 to 0.5
- w_att_out: bfloat16 [128, 128], replicated, may hold values from -0.5 to 0.5
Outputs:
- updated: bfloat16 [1024, 1024, 128], P('rows', 'half')
Inputs may be any that keep to these rules, and one draw needn't show every extreme that they name: The last tokens of the crop are padding, between 102 and 2 * (102) of them: pair_mask[i, k] is 0 wherever token i or token k is padding. Other pairs may be 0 as well.
All inputs are finite; a program needn't handle non-finite values.
Results may differ from a plain program's by a relative error of at most 0.012.
Values may be sent and summed in bfloat16 or wider, within the bound.
No kernel may reach another device: no remote copies, remote signals or barrier semaphores. Data moves between devices by JAX's collectives and lax.ppermute only.
A program may use at most 128 MiB of HBM per device.

v0:
```python
import math
import jax
import jax.numpy as jnp
from jax import lax
from jax.sharding import PartitionSpec as P


def layer_norm(value, gain, axis):
    center = value - jnp.mean(value, axis=axis, keepdims=True)
    spread = jnp.mean(center * center, axis=axis, keepdims=True)
    return center * lax.rsqrt(spread + 1e-05) * gain


def shards(pair, pair_mask, gains, w_tri, w_tri_out, w_att, w_bias, w_att_out):
    rows_here, cols_here, width = pair.shape
    field = pair.astype(jnp.float32)
    normed = layer_norm(field, gains[0], -1).astype(jnp.bfloat16)
    edges = jnp.einsum(
        "ikc,cd->dik", normed, w_tri[:, : 4 * width], preferred_element_type=jnp.float32
    )
    weight_mask = pair_mask.astype(jnp.float32)
    left_edge = (weight_mask * jax.nn.sigmoid(edges[width : 2 * width]) * edges[:width]).astype(
        jnp.bfloat16
    )
    right_edge = (
        weight_mask * jax.nn.sigmoid(edges[3 * width :]) * edges[2 * width : 3 * width]
    ).astype(jnp.bfloat16)
    gate_field = jax.nn.sigmoid(
        jnp.einsum("ikc,cd->ikd", normed, w_tri[:, 4 * width :], preferred_element_type=jnp.float32)
    )
    left_all, right_all = (
        lax.all_to_all(left_edge, "rows", split_axis=0, concat_axis=1, tiled=True),
        lax.all_to_all(right_edge, "rows", split_axis=0, concat_axis=1, tiled=True),
    )
    product = lax.psum_scatter(
        jnp.einsum("cik,cjk->jci", left_all, right_all, preferred_element_type=jnp.float32).astype(
            jnp.bfloat16
        ),
        "half",
        scatter_dimension=0,
        tiled=True,
    )
    returned = lax.all_to_all(product, "rows", split_axis=2, concat_axis=1, tiled=True)
    tri_normed = layer_norm(returned.astype(jnp.float32), gains[1][:, None], 1).astype(jnp.bfloat16)
    update = jnp.einsum("jci,cd->ijd", tri_normed, w_tri_out, preferred_element_type=jnp.float32)
    after_mult = (field + gate_field * update).astype(jnp.bfloat16)
    att_normed = layer_norm(after_mult.astype(jnp.float32), gains[2], -1).astype(jnp.bfloat16)
    projected = jnp.einsum(
        "ijc,cd->ijd", att_normed, w_att, preferred_element_type=jnp.float32
    ).astype(jnp.bfloat16)
    queries = projected[..., :width]
    keys_here = projected[..., width : 2 * width]
    values_here = projected[..., 2 * width : 3 * width]
    gate_attn = projected[..., 3 * width :]
    bias_local = jnp.einsum(
        "ijc,ch->hij", att_normed, w_bias, preferred_element_type=jnp.float32
    ).astype(jnp.bfloat16)
    bias_rows = lax.all_gather(bias_local, "rows", axis=1, tiled=True)
    bias_full = lax.all_gather(bias_rows, "half", axis=2, tiled=True)
    bias_mine = lax.dynamic_slice_in_dim(
        bias_full, lax.axis_index("half") * cols_here, cols_here, 1
    )
    heads = w_bias.shape[1]
    head_dim = width // heads
    scale = head_dim ** (-0.5)
    group = math.gcd(rows_here, 4)
    blocks = rows_here // group
    query_groups = queries.reshape(blocks, group, cols_here, heads, head_dim)
    mask_wire = pair_mask.astype(jnp.bfloat16)
    piece_keys = lax.all_gather(keys_here, "half", axis=1, tiled=True)
    piece_values = lax.all_gather(values_here, "half", axis=1, tiled=True)
    piece_mask = lax.all_gather(mask_wire, "half", axis=1, tiled=True)
    span = piece_keys.shape[1]
    bias_piece = bias_mine.astype(jnp.float32)
    key_groups = piece_keys.reshape(blocks, group, span, heads, head_dim)
    value_groups = piece_values.reshape(blocks, group, span, heads, head_dim)
    mask_groups = piece_mask.astype(jnp.float32).reshape(blocks, group, span)

    def one_block(items):
        query_block, key_block, value_block, mask_block, running, peak, denom = items
        scores = (
            jnp.einsum(
                "gjhd,gkhd->ghjk", query_block, key_block, preferred_element_type=jnp.float32
            )
            * scale
        )
        scores = scores + bias_piece[None]
        scores = jnp.where(mask_block[:, None, None, :] > 0.5, scores, -1000000000.0)
        new_peak = jnp.maximum(peak, jnp.max(scores, axis=-1))
        shrink = jnp.exp(peak - new_peak)
        weights = jnp.exp(scores - new_peak[..., None])
        denom = denom * shrink + jnp.sum(weights, axis=-1)
        running = running * shrink[..., None] + jnp.einsum(
            "ghjk,gkhd->ghjd",
            weights.astype(jnp.bfloat16),
            value_block,
            preferred_element_type=jnp.float32,
        )
        return (running, new_peak, denom)

    running = jnp.zeros((blocks, group, heads, cols_here, head_dim), jnp.float32)
    peak = jnp.full((blocks, group, heads, cols_here), -1e30, jnp.float32)
    denom = jnp.zeros((blocks, group, heads, cols_here), jnp.float32)
    running, peak, denom = lax.map(
        one_block, (query_groups, key_groups, value_groups, mask_groups, running, peak, denom)
    )
    attended = (running / denom[..., None]).reshape(rows_here, heads, cols_here, head_dim)
    attended = jnp.transpose(attended, (0, 2, 1, 3)).reshape(rows_here, cols_here, width)
    gated = (attended * jax.nn.sigmoid(gate_attn.astype(jnp.float32))).astype(jnp.bfloat16)
    output = jnp.einsum("ijc,cd->ijd", gated, w_att_out, preferred_element_type=jnp.float32)
    return (after_mult.astype(jnp.float32) + output).astype(jnp.bfloat16)


def solution(mesh):
    in_specs = (P("rows", "half", None), P("rows", "half"), P(), P(), P(), P(), P(), P())
    out_specs = P("rows", "half", None)
    return jax.shard_map(shards, mesh=mesh, in_specs=in_specs, out_specs=out_specs, check_vma=False)
```

profile of v0, /device:TPU:0, one launch (start us, length us, event | category | flops | bytes accessed | tf_op | source)
XLA Modules:
  0.0 692.3 jit_solution(11790933083862708372)
XLA Ops:
  6.5 3.3 copy.44
  10.2 0.7 fusion.34
  11.0 2.5 convolution_bitcast_fusion
  13.5 3.8 fusion.39
  17.3 4.5 copy.48
  21.9 8.4 %all-to-all-start = ((bf16[128,32,256]{2,1,0:T(8,128)(2,1)}), bf16[128,32,256]{2,1,0:T(8,128)(2,1)}, u32[]{:S(2)}, u32[]{:S(2)}) async-start(bf16[128,32,256]{2,1,0:T(8,128)(2,1)} %copy.48), calls=%async_computation | async-start | bytes 4194304 | tf_op jit(solution)/shard_map/all_to_all | solution.py:33
  30.2 4.7 copy.50
  34.9 25.3 %all-to-all-done = bf16[128,32,256]{2,1,0:T(8,128)(2,1)} async-done(((bf16[128,32,256]{2,1,0:T(8,128)(2,1)}), bf16[128,32,256]{2,1,0:T(8,128)(2,1)}, u32[]{:S(2)}, u32[]{:S(2)}) %all-to-all-start) | async-done | bytes 2097184 | tf_op jit(solution)/shard_map/all_to_all | solution.py:33
  60.2 4.8 all-to-all-start.1
  65.0 3.1 copy.49
  68.2 26.8 %all-to-all-done.1 = bf16[128,32,256]{2,1,0:T(8,128)(2,1)} async-done(((bf16[128,32,256]{2,1,0:T(8,128)(2,1)}), bf16[128,32,256]{2,1,0:T(8,128)(2,1)}, u32[]{:S(2)}, u32[]{:S(2)}) %all-to-all-start.1) | async-done | bytes 2097184 | tf_op jit(solution)/shard_map/all_to_all | solution.py:32
  94.9 1.9 copy.51
  97.1 5.6 convert_bitcast_fusion
  102.8 77.8 %reduce-scatter.2.cloned.1.call-done = bf16[256,4,1024]{2,0,1:T(8,128)(2,1)} async-done(((bf16[1024,4,1024]{2,0,1:T(8,128)(2,1)}), bf16[256,4,1024]{2,0,1:T(8,128)(2,1)}) %reduce-scatter.2.cloned.1.call-update) | async-done | bytes 2097168 | tf_op jit(solution)/shard_map/reduce_scatter | solution.py:35
  180.6 4.2 copy.52
  184.8 35.8 %all_to_all.45 = bf16[256,4,1024]{0,1,2:T(4,128)(2,1)S(1)} all-to-all(bf16[256,4,1024]{0,1,2:T(4,128)(2,1)} %copy.52), channel_id=1, replica_groups=mesh['rows'=32,'half'=4] {'rows'}, dimensions={2} | all-to-all | bytes 4194304 | tf_op jit(solution)/shard_map/all_to_all | solution.py:43
  220.6 0.5 fusion.70
  221.5 0.6 multiply_reduce_fusion
  222.1 0.6 copy.54
  222.7 0.8 fusion.51
  223.5 1.7 fusion.53
  225.2 2.2 convert_reduce_fusion
  227.4 0.7 fusion.31
  228.1 0.6 copy-done.5
  228.7 1.4 fusion.57
  230.1 40.1 %all-gather.7.cloned.1.call-done = bf16[4,1024,256]{2,0,1:T(4,128)(2,1)} async-done(((bf16[4,32,256]{2,0,1:T(4,128)(2,1)}), bf16[4,1024,256]{2,0,1:T(4,128)(2,1)}) %all-gather.7.cloned.1.call-update) | async-done | bytes 2097168 | tf_op jit(solution)/shard_map/all_gather | solution.py:58
  270.3 4.0 convolution_convert_fusion
  274.4 2.9 fusion.69
  277.3 1.6 copy-done.3
  278.9 0.5 all-gather.11.cloned.1.call-update
  279.5 12.6 %all_gather.15 = bf16[32,1024]{1,0:T(8,128)(2,1)S(1)} all-gather(bf16[32,256]{1,0:T(8,128)(2,1)S(1)} %get-tuple-element.101), channel_id=1, replica_groups=mesh['rows'=32,'half'=4] {'half'}, dimensions={1}, use_global_device_ids=true | all-gather | bytes 81920 | tf_op jit(solution)/shard_map/all_gather | solution.py:72
  292.1 67.1 %all-gather.9.cloned.1.call-done = bf16[4,1024,1024]{2,0,1:T(4,128)(2,1)} async-done(((bf16[4,1024,256]{2,0,1:T(4,128)(2,1)}), bf16[4,1024,1024]{2,0,1:T(4,128)(2,1)}) %all-gather.9.cloned.1.call-update) | async-done | bytes 8388624 | tf_op jit(solution)/shard_map/all_gather | solution.py:59
  359.2 2.8 dynamic-slice_convert_fusion
  362.0 4.4 copy.60
  366.4 81.8 %all-gather.5.cloned.1.call-done = bf16[32,1024,128]{1,2,0:T(8,128)(2,1)} async-done(((bf16[32,256,128]{1,2,0:T(8,128)(2,1)}), bf16[32,1024,128]{1,2,0:T(8,128)(2,1)}) %all-gather.5.cloned.1.call-update) | async-done | bytes 8388624 | tf_op jit(solution)/shard_map/all_gather | solution.py:70
  448.2 89.3 %all-gather.11.cloned.1.call-done = bf16[32,1024,128]{1,2,0:T(8,128)(2,1)} async-done(((bf16[32,256,128]{1,2,0:T(8,128)(2,1)}), bf16[32,1024,128]{1,2,0:T(8,128)(2,1)}) %all-gather.11.cloned.1.call-update) | async-done | bytes 8388624 | tf_op jit(solution)/shard_map/all_gather | solution.py:71
  537.5 138.9 %while.12 = (s32[]{:T(128)}, f32[8,4,4,256,32]{3,4,2,1,0:T(8,128)}, f32[8,4,4,256]{3,2,1,0:T(4,128)S(1)}, f32[8,4,1024]{2,1,0:T(4,128)S(1)}, bf16[8,4,256,4,32]{...) while((s32[]{:T(128)}, f32[8,4,4,256,32]{3,4,2,1,0:T(8,128)}, ...), condition=%wide.region_10.11_spmd, body=%wide.region_7.10_spmd.sunk | while | flops 595746816 | bytes 82790528 | solution.py:104
  537.6 5.8 fusion.83
  543.4 5.0 fusion.85
  548.4 6.6 fusion.84
  555.1 5.6 fusion.83
  560.8 5.0 fusion.85
  565.8 6.6 fusion.84
  572.4 5.7 fusion.83
  578.2 5.0 fusion.85
  583.2 6.6 fusion.84
  589.9 5.5 fusion.83
  595.4 5.0 fusion.85
  600.4 6.6 fusion.84
  607.1 5.5 fusion.83
  612.7 5.0 fusion.85
  617.7 6.6 fusion.84
  624.3 5.7 fusion.83
  630.1 5.0 fusion.85
  635.1 6.6 fusion.84
  641.7 5.6 fusion.83
  647.4 5.0 fusion.85
  652.4 6.7 fusion.84
  659.1 5.6 fusion.83
  664.7 5.0 fusion.85
  669.8 6.7 fusion.84
  676.4 3.2 broadcast_divide_fusion
  679.7 3.2 fusion.38
  682.9 2.9 copy.63
  (84 shorter events, 1.9 us)
Async XLA Ops:
  6.5 263.8 %copy-start = (bf16[128,512]{1,0:T(8,128)(2,1)S(1)}, bf16[128,512]{1,0:T(8,128)(2,1)}, u32[]{:S(2)}) copy-start(bf16[128,512]{1,0:T(8,128)(2,1)} %param.15) | copy-start | bytes 393220
  6.5 4.4 copy-start.10
  6.5 4.4 copy-start.9
  6.5 4.5 copy-start.7
  21.9 38.3 %all-to-all-start = ((bf16[128,32,256]{2,1,0:T(8,128)(2,1)}), bf16[128,32,256]{2,1,0:T(8,128)(2,1)}, u32[]{:S(2)}, u32[]{:S(2)}) async-start(bf16[128,32,256]{2,1,0:T(8,128)(2,1)} %copy.48), calls=%async_computation | async-start | bytes 4194304 | tf_op jit(solution)/shard_map/all_to_all | solution.py:33
  60.2 34.7 %all-to-all-start.1 = ((bf16[128,32,256]{2,1,0:T(8,128)(2,1)}), bf16[128,32,256]{2,1,0:T(8,128)(2,1)}, u32[]{:S(2)}, u32[]{:S(2)}) async-start(bf16[128,32,256]{2,1,0:T(8,128)(2,1)} %copy.50), calls=%async_computation.1 | async-start | bytes 4194304 | tf_op jit(solution)/shard_map/all_to_all | solution.py:32
  65.0 115.6 %reduce-scatter.2.cloned.1.call-start = ((), (), s32[]{:S(2)}) async-start(), calls=%async_computation.4 | async-start | bytes 10485760 | tf_op jit(solution)/shard_map/reduce_scatter | solution.py:35
  94.9 2.2 copy-start.4
  102.8 167.5 %all-gather.7.cloned.1.call-start = ((), (), s32[]{:S(2)}) async-start(), calls=%async_computation.6 | async-start | bytes 2162688 | tf_op jit(solution)/shard_map/all_gather | solution.py:58
  222.7 0.8 copy-start.8
  225.2 3.5 copy-start.12
  227.3 1.3 copy-start.5
  230.1 129.1 %all-gather.9.cloned.1.call-start = ((), (), s32[]{:S(2)}) async-start(), calls=%async_computation.7 | async-start | bytes 10485760 | tf_op jit(solution)/shard_map/all_gather | solution.py:59
  270.3 178.0 %all-gather.5.cloned.1.call-start = ((), (), s32[]{:S(2)}) async-start(), calls=%async_computation.5 | async-start | bytes 10485760 | tf_op jit(solution)/shard_map/all_gather | solution.py:70
  274.4 4.5 copy-start.3
  278.9 258.7 %all-gather.11.cloned.1.call-start = ((), (), s32[]{:S(2)}) async-start(), calls=%async_computation.8 | async-start | bytes 10485760 | tf_op jit(solution)/shard_map/all_gather | solution.py:71
  537.6 5.9 copy-start.2
  555.1 5.7 copy-start.2
  572.4 5.8 copy-start.2
  589.9 5.6 copy-start.2
  607.1 5.6 copy-start.2
  624.3 5.8 copy-start.2
  641.7 5.7 copy-start.2
  659.1 5.6 copy-start.2
  676.4 3.2 copy-start.6
  676.4 3.3 copy-start.11
  679.7 6.1 copy-start.1
Sparse Core Ops, SparseCore 0:
  102.9 77.6 reduce-scatter.1
  230.2 40.0 all-gather.6
  271.9 87.2 all-gather.8
  360.7 87.4 all-gather.4
  449.7 87.7 all-gather.10
where the time goes:
time: 693 us; the launch traced here: 692 us
  waiting for transfers between devices  409 us (59%)
  matrix products  119 us (17%)
  other arithmetic  54.1 us (8%)
  blocking collectives  48.4 us (7%)
  local copies, waits for them, and re-layouts  35.1 us (5%)
  between operations  13.4 us (2%)
  starting transfers between devices  13.3 us (2%)
    all_gather x1, waiting for transfers between devices, shards(): piece_values = lax.all_gather(values_here, 'half', axis=1, tiled=True)  89.3 us
    all_gather x1, waiting for transfers between devices, shards(): piece_keys = lax.all_gather(keys_here, 'half', axis=1, tiled=True)  81.8 us
    reduce_scatter x1, waiting for transfers between devices, shards(): lax.psum_scatter(jnp.einsum('cik,cjk->jci', left_all, right_all, preferre...  77.8 us
    all_gather x1, waiting for transfers between devices, shards(): bias_full = lax.all_gather(bias_rows, 'half', axis=2, tiled=True)  67.1 us
    dot_general x8, matrix products, one_block(): jnp.einsum('ghjk,gkhd->ghjd', weights.astype(jnp.bfloat16), value_block,...  53.1 us
    dot_general x8, matrix products, one_block(): jnp.einsum('gjhd,gkhd->ghjk', query_block, key_block, preferred_element_t...  45.2 us
    all_gather x1, waiting for transfers between devices, shards(): bias_rows = lax.all_gather(bias_local, 'rows', axis=1, tiled=True)  40.1 us
    reduce_sum x8, other arithmetic, one_block(): denom = denom * shrink + jnp.sum(weights, axis=-1)  39.8 us
  transfers between devices with their start and end apart: 7, of which 7 were waited for; matrix products, arithmetic and copies ran while one was open for 3% of the time, Pallas kernels for 0%

commit v1 on v0

--- a/solution.py
+++ b/solution.py
@@ -1,8 +1,18 @@
+import functools
 import math
 import jax
 import jax.numpy as jnp
 from jax import lax
 from jax.sharding import PartitionSpec as P
+
+
+def links_spread(mine_x, pos_dim):
+    v1 = jnp.stack(lax.axis_size("rows") * [mine_x])
+    local_out = lax.all_to_all(v1, "rows", 0, 0)
+    return jnp.concatenate(local_out, axis=pos_dim)
+
+
+scan_side = functools.partial(links_spread, pos_dim=1)
 
 
 def layer_norm(value, gain, axis):
@@ -55,7 +65,7 @@
     bias_local = jnp.einsum(
         "ijc,ch->hij", att_normed, w_bias, preferred_element_type=jnp.float32
     ).astype(jnp.bfloat16)
-    bias_rows = lax.all_gather(bias_local, "rows", axis=1, tiled=True)
+    bias_rows = scan_side(bias_local)
     bias_full = lax.all_gather(bias_rows, "half", axis=2, tiled=True)
     bias_mine = lax.dynamic_slice_in_dim(
         bias_full, lax.axis_index("half") * cols_here, cols_here, 1

time: 693 us -> 686 us (0.990)
  waiting for transfers between devices: 409 us -> 367 us
  blocking collectives: 48.4 us -> 80 us
    all_gather x1 -> x0, waiting for transfers between devices: 40.1 us -> none  [shards(): bias_rows = lax.all_gather(bias_local, 'rows', axis=1, tiled=True)]
    all_to_all x0 -> x1, blocking collectives: none -> 31.9 us  [links_spread(): local_out = lax.all_to_all(v1, 'rows', 0, 0)]
  transfers between devices with their start and end apart: 7 -> 6, of which waited for: 7 -> 6; matrix products, arithmetic and copies ran while one was open for 3% -> 3% of each run, Pallas kernels for 0% -> 0%
where the time goes in v1:
time: 686 us; the launch traced here: 685 us
  waiting for transfers between devices  367 us (53%)
  matrix products  121 us (18%)
  blocking collectives  80 us (12%)
  other arithmetic  55.2 us (8%)
  local copies, waits for them, and re-layouts  35.5 us (5%)
  between operations  13.4 us (2%)
  starting transfers between devices  13.3 us (2%)
    all_gather x1, waiting for transfers between devices, shards(): piece_values = lax.all_gather(values_here, 'half', axis=1, tiled=True)  89.3 us
    all_gather x1, waiting for transfers between devices, shards(): piece_keys = lax.all_gather(keys_here, 'half', axis=1, tiled=True)  85.3 us
    reduce_scatter x1, waiting for transfers between devices, shards(): lax.psum_scatter(jnp.einsum('cik,cjk->jci', left_all, right_all, preferre...  77.8 us
    all_gather x1, waiting for transfers between devices, shards(): bias_full = lax.all_gather(bias_rows, 'half', axis=2, tiled=True)  61.8 us
    dot_general x8, matrix products, one_block(): jnp.einsum('ghjk,gkhd->ghjd', weights.astype(jnp.bfloat16), value_block,...  53 us
    dot_general x8, matrix products, one_block(): jnp.einsum('gjhd,gkhd->ghjk', query_block, key_block, preferred_element_t...  47.9 us
    reduce_sum x8, other arithmetic, one_block(): denom = denom * shrink + jnp.sum(weights, axis=-1)  39.8 us
    all_to_all x1, blocking collectives, shards(): lax.all_to_all(product, 'rows', split_axis=2, concat_axis=1, tiled=True)  35.8 us
  transfers between devices with their start and end apart: 6, of which 6 were waited for; matrix products, arithmetic and copies ran while one was open for 3% of the time, Pallas kernels for 0%

profile of v1, /device:TPU:0, one launch (start us, length us, event | category | flops | bytes accessed | tf_op | source)
XLA Modules:
  0.0 685.3 jit_solution(9243901974992180033)
XLA Ops:
  6.5 3.3 copy.64
  10.2 0.7 fusion.34
  11.0 2.5 convolution_bitcast_fusion
  13.5 3.8 fusion.39
  17.3 4.5 copy.68
  21.8 8.4 %all-to-all-start = ((bf16[128,32,256]{2,1,0:T(8,128)(2,1)}), bf16[128,32,256]{2,1,0:T(8,128)(2,1)}, u32[]{:S(2)}, u32[]{:S(2)}) async-start(bf16[128,32,256]{2,1,0:T(8,128)(2,1)} %copy.68), calls=%async_computation | async-start | bytes 4194304 | tf_op jit(solution)/shard_map/all_to_all | solution.py:43
  30.2 4.6 copy.70
  34.8 25.3 %all-to-all-done = bf16[128,32,256]{2,1,0:T(8,128)(2,1)} async-done(((bf16[128,32,256]{2,1,0:T(8,128)(2,1)}), bf16[128,32,256]{2,1,0:T(8,128)(2,1)}, u32[]{:S(2)}, u32[]{:S(2)}) %all-to-all-start) | async-done | bytes 2097184 | tf_op jit(solution)/shard_map/all_to_all | solution.py:43
  60.2 4.8 all-to-all-start.1
  65.0 3.1 copy.69
  68.1 26.8 %all-to-all-done.1 = bf16[128,32,256]{2,1,0:T(8,128)(2,1)} async-done(((bf16[128,32,256]{2,1,0:T(8,128)(2,1)}), bf16[128,32,256]{2,1,0:T(8,128)(2,1)}, u32[]{:S(2)}, u32[]{:S(2)}) %all-to-all-start.1) | async-done | bytes 2097184 | tf_op jit(solution)/shard_map/all_to_all | solution.py:42
  94.9 1.9 copy.71
  97.1 5.6 convert_bitcast_fusion
  102.8 77.8 %reduce-scatter.2.cloned.1.call-done = bf16[256,4,1024]{2,0,1:T(8,128)(2,1)} async-done(((bf16[1024,4,1024]{2,0,1:T(8,128)(2,1)}), bf16[256,4,1024]{2,0,1:T(8,128)(2,1)}) %reduce-scatter.2.cloned.1.call-update) | async-done | bytes 2097168 | tf_op jit(solution)/shard_map/reduce_scatter | solution.py:45
  180.6 4.2 copy.72
  184.8 35.8 %all_to_all.50 = bf16[256,4,1024]{0,1,2:T(4,128)(2,1)S(1)} all-to-all(bf16[256,4,1024]{0,1,2:T(4,128)(2,1)} %copy.72), channel_id=1, replica_groups=mesh['rows'=32,'half'=4] {'rows'}, dimensions={2} | all-to-all | bytes 4194304 | tf_op jit(solution)/shard_map/all_to_all | solution.py:53
  220.6 0.5 fusion.70
  221.4 0.6 multiply_reduce_fusion
  222.1 0.6 copy.74
  222.7 0.8 fusion.51
  223.5 1.6 fusion.53
  225.1 2.2 convert_reduce_fusion
  227.3 0.7 fusion.31
  228.0 0.7 fusion.57
  229.1 31.9 %all_to_all.51 = bf16[32,4,32,256]{3,2,1,0:T(8,128)(2,1)S(1)} all-to-all(bf16[32,4,32,256]{3,2,1,0:T(8,128)(2,1)S(1)} %stack.2), channel_id=1, replica_groups=mesh['rows'=32,'half'=4] {'rows'}, dimensions={0} | all-to-all | bytes 4194304 | tf_op jit(solution)/shard_map/all_to_all | solution.py:11
  261.0 1.5 copy.81
  262.6 0.8 copy-done.6
  263.3 2.5 convolution_convert_fusion
  265.8 2.8 fusion.69
  268.7 3.3 copy-done.3
  272.1 0.5 all-gather.8.cloned.1.call-update
  272.6 12.3 %all_gather.12 = bf16[32,1024]{1,0:T(8,128)(2,1)S(1)} all-gather(bf16[32,256]{1,0:T(8,128)(2,1)S(1)} %get-tuple-element.77), channel_id=1, replica_groups=mesh['rows'=32,'half'=4] {'half'}, dimensions={1}, use_global_device_ids=true | all-gather | bytes 81920 | tf_op jit(solution)/shard_map/all_gather | solution.py:82
  284.9 61.8 %all-gather.6.cloned.1.call-done = bf16[4,1024,1024]{2,1,0:T(8,128)(2,1)} async-done(((bf16[4,1024,256]{2,1,0:T(8,128)(2,1)}), bf16[4,1024,1024]{2,1,0:T(8,128)(2,1)}) %all-gather.6.cloned.1.call-update) | async-done | bytes 8388624 | tf_op jit(solution)/shard_map/all_gather | solution.py:69
  346.8 4.1 dynamic-slice_convert_fusion
  350.9 85.3 %all-gather.4.cloned.1.call-done = bf16[32,1024,128]{1,2,0:T(8,128)(2,1)} async-done(((bf16[32,256,128]{1,2,0:T(8,128)(2,1)}), bf16[32,1024,128]{1,2,0:T(8,128)(2,1)}) %all-gather.4.cloned.1.call-update) | async-done | bytes 8388624 | tf_op jit(solution)/shard_map/all_gather | solution.py:80
  436.1 89.3 %all-gather.8.cloned.1.call-done = bf16[32,1024,128]{1,2,0:T(8,128)(2,1)} async-done(((bf16[32,256,128]{1,2,0:T(8,128)(2,1)}), bf16[32,1024,128]{1,2,0:T(8,128)(2,1)}) %all-gather.8.cloned.1.call-update) | async-done | bytes 8388624 | tf_op jit(solution)/shard_map/all_gather | solution.py:81
  525.5 141.5 %while.12 = (s32[]{:T(128)}, f32[8,4,4,256,32]{3,4,2,1,0:T(8,128)}, f32[8,4,4,256]{3,2,1,0:T(4,128)S(1)}, f32[8,4,1024]{2,1,0:T(4,128)S(1)}, bf16[8,4,256,4,32]{...) while((s32[]{:T(128)}, f32[8,4,4,256,32]{3,4,2,1,0:T(8,128)}, ...), condition=%wide.region_10.11_spmd, body=%wide.region_7.10_spmd.sunk | while | flops 595746816 | bytes 82790528 | solution.py:114
  525.5 6.0 fusion.83
  531.5 5.0 fusion.85
  536.5 6.6 fusion.84
  543.2 6.0 fusion.83
  549.2 5.0 fusion.85
  554.2 6.6 fusion.84
  560.8 6.0 fusion.83
  566.9 5.0 fusion.85
  571.9 6.6 fusion.84
  578.5 6.0 fusion.83
  584.6 5.0 fusion.85
  589.6 6.6 fusion.84
  596.2 6.0 fusion.83
  602.2 5.0 fusion.85
  607.3 6.6 fusion.84
  613.9 6.0 fusion.83
  619.9 5.0 fusion.85
  625.0 6.6 fusion.84
  631.6 6.0 fusion.83
  637.7 5.0 fusion.85
  642.7 6.6 fusion.84
  649.3 6.0 fusion.83
  655.4 5.0 fusion.85
  660.4 6.6 fusion.84
  667.0 3.1 broadcast_divide_fusion
  670.1 4.6 fusion.38
  674.7 4.1 copy.84
  (84 shorter events, 2.1 us)
Async XLA Ops:
  6.5 256.0 %copy-start = (bf16[128,512]{1,0:T(8,128)(2,1)S(1)}, bf16[128,512]{1,0:T(8,128)(2,1)}, u32[]{:S(2)}) copy-start(bf16[128,512]{1,0:T(8,128)(2,1)} %param.15) | copy-start | bytes 393220
  6.5 4.4 copy-start.10
  6.5 4.4 copy-start.9
  6.5 4.5 copy-start.7
  21.8 38.3 %all-to-all-start = ((bf16[128,32,256]{2,1,0:T(8,128)(2,1)}), bf16[128,32,256]{2,1,0:T(8,128)(2,1)}, u32[]{:S(2)}, u32[]{:S(2)}) async-start(bf16[128,32,256]{2,1,0:T(8,128)(2,1)} %copy.68), calls=%async_computation | async-start | bytes 4194304 | tf_op jit(solution)/shard_map/all_to_all | solution.py:43
  60.2 34.7 %all-to-all-start.1 = ((bf16[128,32,256]{2,1,0:T(8,128)(2,1)}), bf16[128,32,256]{2,1,0:T(8,128)(2,1)}, u32[]{:S(2)}, u32[]{:S(2)}) async-start(bf16[128,32,256]{2,1,0:T(8,128)(2,1)} %copy.70), calls=%async_computation.1 | async-start | bytes 4194304 | tf_op jit(solution)/shard_map/all_to_all | solution.py:42
  64.9 115.6 %reduce-scatter.2.cloned.1.call-start = ((), (), s32[]{:S(2)}) async-start(), calls=%async_computation.5 | async-start | bytes 10485760 | tf_op jit(solution)/shard_map/reduce_scatter | solution.py:45
  94.9 2.2 copy-start.4
  102.7 244.0 %all-gather.6.cloned.1.call-start = ((), (), s32[]{:S(2)}) async-start(), calls=%async_computation.7 | async-start | bytes 10485760 | tf_op jit(solution)/shard_map/all_gather | solution.py:69
  222.6 0.8 copy-start.8
  225.1 2.9 copy-start.12
  227.3 1.8 copy-start.5
  261.0 2.3 copy-start.6
  262.5 173.6 %all-gather.4.cloned.1.call-start = ((), (), s32[]{:S(2)}) async-start(), calls=%async_computation.6 | async-start | bytes 10485760 | tf_op jit(solution)/shard_map/all_gather | solution.py:80
  265.8 6.2 copy-start.3
  272.0 253.5 %all-gather.8.cloned.1.call-start = ((), (), s32[]{:S(2)}) async-start(), calls=%async_computation.8 | async-start | bytes 10485760 | tf_op jit(solution)/shard_map/all_gather | solution.py:81
  525.5 6.0 copy-start.2
  543.1 6.0 copy-start.2
  560.8 6.0 copy-start.2
  578.5 6.0 copy-start.2
  596.2 6.0 copy-start.2
  613.9 6.0 copy-start.2
  631.6 6.0 copy-start.2
  649.3 6.0 copy-start.2
  667.0 3.1 copy-start.11
  670.1 8.7 %copy-start.1 = (bf16[128,512]{1,0:T(8,128)(2,1)S(1)}, bf16[128,512]{1,0:T(8,128)(2,1)}, u32[]{:S(2)}) copy-start(bf16[128,512]{1,0:T(8,128)(2,1)} %param.15) | copy-start | bytes 393220
Sparse Core Ops, SparseCore 0:
  102.9 77.6 reduce-scatter.1
  262.6 84.0 all-gather.5
  348.4 87.6 all-gather.3
  437.6 87.7 all-gather.7
